TPU v7x, 32 devices: a whole 2x2x4 slice. The times are simulated.
32 devices in a mesh: row: 16 (over z, y, core), col: 2 (over x).
Axes of the slice: x: 2, y: 2, z: 4, core: 2. Of those that a mesh axis runs over, the one named last changes fastest.
Arguments:
- features: bfloat16 [16384, 128], P(('col', 'row')), may hold values from -6 to 6
- weight: bfloat16 [128, 172], replicated, may hold values from -0.5 to 0.5
- labels: int32 [16384], P(('row', 'col')), may hold values from -43 to 171
- tile_rows: int32 [16, 2, 256], P('row', 'col'), may hold values from 0 to 7, as said below
- tile_cols: int32 [16, 2, 256], P('row', 'col'), may hold values from 0 to 63
- tile_count: int32 [16, 2], P('row', 'col'), may hold values from 1 to 256, as said below
- tile_vals: bfloat16 [16, 2, 256, 128, 128], P('row', 'col'), may hold values from -0.07470703 to 0.07470703
Outputs:
- logits: float32 [16384, 172], P(('row', 'col'))
- weight_grad: float32 [128, 172], replicated
Inputs may be any that keep to these rules, and one draw needn't show every extreme that they name: `tile_rows`: within one device the used slots name distinct tiles; unused slots are ignored. `tile_count`: counts differ between devices; in every draw some device uses all 256 slots.
All inputs are finite; a program needn't handle non-finite values.
Results may differ from a plain program's by a relative error of at most 0.0029.
Values may be sent and summed in bfloat16 or wider, within the bound.
A program may use at most 128 MiB of HBM per device.

v0:
```python
import jax
import jax.numpy as jnp
from jax import lax
from jax.sharding import PartitionSpec as P


def aggregate(table, gather_idx, scatter_idx, vals, count, out_tiles, transpose):
    blk = min(32, vals.shape[0])
    classes = table.shape[-1]
    nblk = (count + blk - 1) // blk

    def step(b, acc):
        start = (b * blk).astype(jnp.int32)
        piece = lax.dynamic_slice_in_dim(vals, start, blk, 0)
        gidx = lax.dynamic_slice_in_dim(gather_idx, start, blk, 0)
        sidx = lax.dynamic_slice_in_dim(scatter_idx, start, blk, 0)
        sel = table[gidx]
        if transpose:
            prod = jnp.einsum("tji,tjc->tic", piece, sel, preferred_element_type=jnp.float32)
        else:
            prod = jnp.einsum("tij,tjc->tic", piece, sel, preferred_element_type=jnp.float32)
        valid = (start + jnp.arange(blk, dtype=jnp.int32) < count).astype(jnp.float32)
        return acc.at[sidx].add(prod * valid[:, None, None])

    init = jnp.zeros((out_tiles, table.shape[1], classes), jnp.float32)
    return lax.fori_loop(0, nblk, step, init)


def split_product(inputs, grads):
    upper = lax.optimization_barrier(grads.astype(jnp.bfloat16))
    lower = (grads - upper.astype(jnp.float32)).astype(jnp.bfloat16)
    first = jnp.einsum("nf,nc->fc", inputs, upper, preferred_element_type=jnp.float32)
    second = jnp.einsum("nf,nc->fc", inputs, lower, preferred_element_type=jnp.float32)
    return first + second


def local(features, weight, labels, tile_rows, tile_cols, tile_count, tile_vals):
    classes = weight.shape[1]
    tile = tile_vals.shape[-1]
    slots = tile_vals.shape[2]
    vals = tile_vals.reshape(slots, tile, tile)
    rows_idx = tile_rows.reshape(slots)
    cols_idx = tile_cols.reshape(slots)
    count = tile_count.reshape(())
    row_tiles = lax.axis_size("col") * features.shape[0] // tile
    nodes = features.shape[0] * lax.axis_size("row") * lax.axis_size("col")
    local_xw = jnp.dot(features, weight, preferred_element_type=jnp.float32).astype(jnp.bfloat16)
    xw_full = lax.all_gather(local_xw, "row", axis=0, tiled=True)
    table = xw_full.reshape(-1, tile, classes)
    col_tiles = table.shape[0]
    partial_value = aggregate(table, cols_idx, rows_idx, vals, count, row_tiles, False)
    logits = lax.psum_scatter(
        partial_value.reshape(-1, classes), "col", scatter_dimension=0, tiled=True
    )
    onehot = (labels[:, None] == jnp.arange(classes, dtype=jnp.int32)[None, :]).astype(jnp.float32)
    residual_grad = jnp.where(labels[:, None] >= 0, logits - onehot, 0.0).astype(jnp.bfloat16)
    loss_full = lax.all_gather(residual_grad, "col", axis=0, tiled=True)
    back = aggregate(
        loss_full.reshape(-1, tile, classes), rows_idx, cols_idx, vals, count, col_tiles, True
    )
    projected_grad = lax.psum_scatter(
        back.reshape(-1, classes), "row", scatter_dimension=0, tiled=True
    )
    local_grad = split_product(features, projected_grad)
    total_grad = lax.psum(local_grad, ("row", "col"))
    weight_grad = total_grad / jnp.sqrt(jnp.float32(nodes))
    return (logits, weight_grad)


def solution(mesh):
    placed = (
        P(("col", "row"), None),
        P(),
        P(("row", "col")),
        P("row", "col", None),
        P("row", "col", None),
        P("row", "col"),
        P("row", "col", None, None, None),
    )
    return jax.shard_map(
        local, mesh=mesh, in_specs=placed, out_specs=(P(("row", "col"), None), P()), check_vma=False
    )
```

profile of v0, /device:TPU:0, one launch (start us, length us, event | category | flops | bytes accessed | tf_op | source)
XLA Modules:
  0.0 520.8 jit_solution(3133843167572993465)
XLA Ops:
  7.2 0.8 copy-done
  8.1 1.7 convolution_convert_fusion
  10.5 48.6 %all-gather.2.cloned.1.call-done = bf16[8192,172]{0,1:T(8,128)(2,1)} async-done(((bf16[512,172]{0,1:T(8,128)(2,1)}), bf16[8192,172]{0,1:T(8,128)(2,1)}) %all-gather.2.cloned.1.call-update) | async-done | bytes 2818064 | tf_op jit(solution)/shard_map/all_gather | solution.py:48
  59.1 5.8 %copy.22 = bf16[8192,172]{1,0:T(8,128)(2,1)} copy(bf16[8192,172]{0,1:T(8,128)(2,1)} %all-gather.2.cloned.1.call-done) | data formatting | bytes 5636096 | tf_op jit(solution)/shard_map/while | solution.py:26
  65.0 38.0 %while.20 = (s32[]{:T(128)}, f32[8,128,172]{1,2,0:T(8,128)S(1)}, s32[]{:T(128)}, s32[256]{0:T(256)S(1)}, bf16[256,128,128]{2,1,0:T(8,128)(2,1)}, /*index=5*/s32[...) while((s32[]{:T(128)}, f32[8,128,172]{1,2,0:T(8,128)S(1)}, ...), condition=%wide.region_2.3_spmd, body=%wide.region_0.2_spmd.sunk | while | flops 181765408 | bytes 16553267 | solution.py:26
  65.0 0.7 compare_convert_fusion.4
  65.8 2.9 gather_fusion
  68.6 3.7 convolution_multiply_fusion.4
  72.3 5.3 %scatter_fusion = f32[8,128,172]{1,2,0:T(8,128)S(1)} fusion(f32[8,128,172]{1,2,0:T(8,128)S(1)} %get-tuple-element.279, s32[32]{0:T(128)S(1)} %get-tuple-element.254, f32[32,128,172]{1,2,0:T(8,128)} %convolution_multiply_fusion.4), kind=kCustom, calls=%fused_computation.2.clone.1 | custom fusion | flops 704512 | bytes 8454272 | tf_op jit(solution)/shard_map/while/body/scatter-add | solution.py:23
  77.7 0.7 compare_convert_fusion.4
  78.3 0.1 compare_select_fusion.6
  78.4 2.9 gather_fusion
  81.3 3.7 convolution_multiply_fusion.4
  84.9 5.3 %scatter_fusion = f32[8,128,172]{1,2,0:T(8,128)S(1)} fusion(f32[8,128,172]{1,2,0:T(8,128)S(1)} %get-tuple-element.279, s32[32]{0:T(128)S(1)} %get-tuple-element.254, f32[32,128,172]{1,2,0:T(8,128)} %convolution_multiply_fusion.4), kind=kCustom, calls=%fused_computation.2.clone.1 | custom fusion | flops 704512 | bytes 8454272 | tf_op jit(solution)/shard_map/while/body/scatter-add | solution.py:23
  90.3 0.7 compare_convert_fusion.4
  91.0 0.1 compare_select_fusion.6
  91.1 2.9 gather_fusion
  93.9 3.7 convolution_multiply_fusion.4
  97.6 5.3 %scatter_fusion = f32[8,128,172]{1,2,0:T(8,128)S(1)} fusion(f32[8,128,172]{1,2,0:T(8,128)S(1)} %get-tuple-element.279, s32[32]{0:T(128)S(1)} %get-tuple-element.254, f32[32,128,172]{1,2,0:T(8,128)} %convolution_multiply_fusion.4), kind=kCustom, calls=%fused_computation.2.clone.1 | custom fusion | flops 704512 | bytes 8454272 | tf_op jit(solution)/shard_map/while/body/scatter-add | solution.py:23
  103.0 0.2 copy.29
  103.3 1.0 copy.24
  104.4 77.2 %reduce-scatter.3.cloned.1.call-done = f32[512,172]{0,1:T(8,128)} async-done(((f32[1024,172]{0,1:T(8,128)}), f32[512,172]{0,1:T(8,128)}) %reduce-scatter.3.cloned.1.call-update) | async-done | bytes 352272 | tf_op jit(solution)/shard_map/reduce_scatter | solution.py:52
  181.6 1.0 select_convert_fusion
  182.6 7.0 %all_gather.7 = bf16[1024,172]{0,1:T(8,128)(2,1)S(1)} all-gather(bf16[512,172]{0,1:T(8,128)(2,1)S(1)} %select_convert_fusion), channel_id=1, replica_groups=mesh['row'=16,'col'=2] {'col'}, dimensions={0}, use_global_device_ids=true | all-gather | bytes 528384 | tf_op jit(solution)/shard_map/all_gather | solution.py:57
  189.6 0.2 copy.23
  189.8 2.9 broadcast_in_dim.36
  192.7 38.2 %while.21 = (s32[]{:T(128)}, f32[64,128,172]{1,2,0:T(8,128)}, s32[]{:T(128)}, s32[256]{0:T(256)S(1)}, bf16[256,128,128]{2,1,0:T(8,128)(2,1)}, /*index=5*/s32[256...) while((s32[]{:T(128)}, f32[64,128,172]{1,2,0:T(8,128)}, ...), condition=%wide.region_6.7_spmd, body=%wide.region_4.6_spmd.sunk | while | flops 181765408 | bytes 17241396 | solution.py:26
  192.7 0.6 compare_convert_fusion.5
  193.4 2.0 gather_fusion.1
  195.4 2.8 convolution_multiply_fusion.5
  198.2 7.1 %scatter_fusion.1 = f32[64,128,172]{1,2,0:T(8,128)} fusion(f32[64,128,172]{1,2,0:T(8,128)} %get-tuple-element.315, s32[32]{0:T(128)S(1)} %get-tuple-element.264, f32[32,128,172]{1,2,0:T(8,128)S(1)} %convolution_multiply_fusion.5), kind=kCustom, calls=%fused_computation.3.clone.1 | custom fusion | flops 704512 | bytes 8454272 | tf_op jit(solution)/shard_map/while/body/scatter-add | solution.py:23
  205.3 0.6 compare_convert_fusion.5
  206.1 2.0 gather_fusion.1
  208.0 2.8 convolution_multiply_fusion.5
  210.9 7.2 %scatter_fusion.1 = f32[64,128,172]{1,2,0:T(8,128)} fusion(f32[64,128,172]{1,2,0:T(8,128)} %get-tuple-element.315, s32[32]{0:T(128)S(1)} %get-tuple-element.264, f32[32,128,172]{1,2,0:T(8,128)S(1)} %convolution_multiply_fusion.5), kind=kCustom, calls=%fused_computation.3.clone.1 | custom fusion | flops 704512 | bytes 8454272 | tf_op jit(solution)/shard_map/while/body/scatter-add | solution.py:23
  218.1 0.6 compare_convert_fusion.5
  218.8 2.0 gather_fusion.1
  220.8 2.8 convolution_multiply_fusion.5
  223.6 7.2 %scatter_fusion.1 = f32[64,128,172]{1,2,0:T(8,128)} fusion(f32[64,128,172]{1,2,0:T(8,128)} %get-tuple-element.315, s32[32]{0:T(128)S(1)} %get-tuple-element.264, f32[32,128,172]{1,2,0:T(8,128)S(1)} %convolution_multiply_fusion.5), kind=kCustom, calls=%fused_computation.3.clone.1 | custom fusion | flops 704512 | bytes 8454272 | tf_op jit(solution)/shard_map/while/body/scatter-add | solution.py:23
  230.8 4.4 copy.28
  235.3 0.9 pad.3
  236.2 7.4 %copy.25 = f32[22,8,64,128]{3,1,2,0:T(8,128)} copy(f32[22,8,64,128]{3,2,1,0:T(8,128)S(1)} %bitcast.37) | data formatting | bytes 11534336
  243.7 142.8 %reduce-scatter.5.cloned.1.call-done = f32[512,172]{0,1:T(8,128)} async-done(((f32[8192,172]{0,1:T(8,128)}), f32[512,172]{0,1:T(8,128)}) %reduce-scatter.5.cloned.1.call-update) | async-done | bytes 352272 | tf_op jit(solution)/shard_map/reduce_scatter | solution.py:61
  386.5 1.0 convert_element_type.35
  387.6 0.2 fusion.5
  387.8 1.8 fusion.4
  389.6 123.1 %all-reduce.2.cloned.1.call-done = f32[128,172]{0,1:T(8,128)} async-done(((f32[128,172]{0,1:T(8,128)}), f32[128,172]{0,1:T(8,128)}) %all-reduce.2.cloned.1.call-update) | async-done | bytes 88080 | tf_op jit(solution)/shard_map/psum | solution.py:65
  512.7 1.5 broadcast_multiply_fusion
  (28 shorter events, 0.7 us)
Async XLA Ops:
  7.2 0.9 copy-start
  7.2 52.0 %all-gather.2.cloned.1.call-start = ((), (), s32[]{:S(2)}) async-start(), calls=%async_computation.2 | async-start | bytes 3063808 | tf_op jit(solution)/shard_map/all_gather | solution.py:48
  9.8 171.8 %reduce-scatter.3.cloned.1.call-start = ((), (), s32[]{:S(2)}) async-start(), calls=%async_computation.3 | async-start | bytes 1081344 | tf_op jit(solution)/shard_map/reduce_scatter | solution.py:52
  10.5 54.5 %copy-start.1 = (s32[1,1,256]{2,1,0:T(1,128)S(1)}, s32[1,1,256]{2,1,0:T(1,128)}, u32[]{:S(2)}) copy-start(s32[1,1,256]{2,1,0:T(1,128)} %param.14) | copy-start | bytes 3076
  10.5 54.5 %copy-start.2 = (s32[1,1,256]{2,1,0:T(1,128)S(1)}, s32[1,1,256]{2,1,0:T(1,128)}, u32[]{:S(2)}) copy-start(s32[1,1,256]{2,1,0:T(1,128)} %param.15) | copy-start | bytes 3076
  103.0 1.4 copy-start.3
  104.3 282.3 %reduce-scatter.5.cloned.1.call-start = ((), (), s32[]{:S(2)}) async-start(), calls=%async_computation.4 | async-start | bytes 6127616 | tf_op jit(solution)/shard_map/reduce_scatter | solution.py:61
  243.7 269.0 %all-reduce.2.cloned.1.call-start = ((), (), s32[]{:S(2)}) async-start(), calls=%async_computation.5 | async-start | bytes 180224 | tf_op jit(solution)/shard_map/psum | solution.py:65
Sparse Core Ops, SparseCore 0:
  10.7 48.3 all-gather.1
  104.4 77.1 reduce-scatter.2
  243.8 142.7 reduce-scatter.4
  393.5 119.1 all-reduce.1
where the time goes:
time: 523 us; the launch traced here: 521 us
  waiting for transfers between devices  392 us (75%)
  other arithmetic  45.6 us (9%)
  local copies, waits for them, and re-layouts  38.4 us (7%)
  matrix products  23.1 us (4%)
  between operations  14.6 us (3%)
  blocking collectives  6.97 us (1%)
    reduce_scatter x1, waiting for transfers between devices, local(): lax.psum_scatter(back.reshape(-1, classes), 'row', scatter_dimension=0, t...  143 us
    psum x1, waiting for transfers between devices, local(): total_grad = lax.psum(local_grad, ('row', 'col'))  123 us
    reduce_scatter x1, waiting for transfers between devices, local(): lax.psum_scatter(partial_value.reshape(-1, classes), 'col', scatter_dimen...  77.2 us
    all_gather x1, waiting for transfers between devices, local(): xw_full = lax.all_gather(local_xw, 'row', axis=0, tiled=True)  48.6 us
    scatter-add x6, other arithmetic, step(): return acc.at[sidx].add(prod * valid[:, None, None])  37.5 us
    gather x6, local copies, waits for them, and re-layouts, step(): sel = table[gidx]  14.6 us
    dot_general x3, matrix products, step(): jnp.einsum('tij,tjc->tic', piece, sel, preferred_element_type=jnp.float32)  11 us
    while x4, local copies, waits for them, and re-layouts, aggregate(): return lax.fori_loop(0, nblk, step, init)  10.7 us
  transfers between devices with their start and end apart: 4, of which 4 were waited for; matrix products, arithmetic and copies ran while one was open for 0% of the time, Pallas kernels for 0%

commit v1 on v0

v1 whole, which is shorter than its diff:
```python
import functools
import math

import jax
import jax.numpy as jnp
from jax import lax
from jax.experimental import pallas as pl
from jax.experimental.pallas import tpu as pltpu
from jax.sharding import PartitionSpec as P

F32, BF16 = jnp.float32, jnp.bfloat16
MESH = pl.DeviceIdType.MESH


def factors(n_row):
    cores = 2 if n_row % 2 == 0 else 1
    chips = n_row // cores
    la = 4 if chips % 4 == 0 else chips
    return la, chips // la, cores


def nearest(pos, size, n):
    out = 0
    for p in range(size):
        order = sorted(range(size), key=lambda s: (abs(s - p), s))
        out = out + jnp.where(pos == p, order[n], 0)
    return out


def split(x):
    hi = x.astype(BF16)
    return hi, (x - hi.astype(F32)).astype(BF16)


def dot(a, b):
    return jnp.dot(a, b, preferred_element_type=F32)


def kernel(dims, feat, weight, labels, tab, vals, logits, wgrad,
           x, tiles, acc1, acc2, out2, in1, in2,
           ssem, rsem, vsem, s1, r1, s2, r2):
    n_row, n_col, la, lb, cores, scale = dims
    slots, tile = vals.shape[0], vals.shape[1]
    rt, bt = acc1.shape[0], feat.shape[0] // tile
    ct = n_row * bt
    row, col = lax.axis_index("row"), lax.axis_index("col")
    core = row % cores
    q = (row // cores) % lb
    p = row // (cores * lb)

    def place(s, t, c):
        return (s * lb + t) * cores + c

    def when(cond, fn):
        if cond is True:
            fn()
        else:
            pl.when(cond)(fn)

    fetch = pltpu.make_async_copy(vals, tiles.at[pl.ds(0, slots)], vsem)
    fetch.start()

    barrier = pltpu.get_barrier_semaphore()
    peers = [(p + 1 < la, place(p + 1, q, core)), (p > 0, place(p - 1, q, core)),
             (q + 1 < lb, place(p, q + 1, core)), (q > 0, place(p, q - 1, core))]
    if cores == 2:
        peers.append((True, place(p, q, 1 - core)))
    for cond, where in peers:
        when(cond, functools.partial(pl.semaphore_signal, barrier, inc=1, device_id={"row": where}, device_id_type=MESH))
    for k in range(1, n_col):
        pl.semaphore_signal(barrier, inc=1, device_id={"col": (col + k) % n_col}, device_id_type=MESH)
    x[row] = feat[...]
    tiles[slots] = jnp.zeros((tile, tile), BF16)
    count = n_col - 1 + (cores - 1)
    for cond, _ in peers[:4]:
        count = count + jnp.where(cond, 1, 0)
    pl.semaphore_wait(barrier, count)

    started = []

    def send(cond, step, way, block, where):
        copy = pltpu.make_async_remote_copy(
            src_ref=x.at[block], dst_ref=x.at[block], send_sem=ssem.at[step, way], recv_sem=rsem.at[block],
            device_id={"row": where}, device_id_type=MESH)
        when(cond, copy.start)
        started.append((cond, copy))

    def arrive(block):
        pltpu.make_async_remote_copy(
            src_ref=x.at[block], dst_ref=x.at[block], send_sem=ssem.at[0, 0], recv_sem=rsem.at[block],
            device_id={"row": (row + 1) % n_row}, device_id_type=MESH).wait_recv()

    def forward(na, nb, s, t):
        block, step = place(s, t, core), na * lb + nb
        if nb == 0:
            up = p + 1 < la if na == 0 else jnp.logical_and(s < p, p + 1 < la)
            down = p > 0 if na == 0 else jnp.logical_and(s > p, p > 0)
            send(up, step, 0, block, place(p + 1, q, core))
            send(down, step, 1, block, place(p - 1, q, core))
            send(q + 1 < lb, step, 2, block, place(p, q + 1, core))
            send(q > 0, step, 3, block, place(p, q - 1, core))
        elif lb > 2:
            send(jnp.logical_and(t < q, q + 1 < lb), step, 2, block, place(p, q + 1, core))
            send(jnp.logical_and(t > q, q > 0), step, 3, block, place(p, q - 1, core))
        if cores == 2:
            send(True, step, 4, block, place(p, q, 1 - core))

    def multiply(block, acc, lo, hi, first=False):
        def body(n, carry):
            i = ((col + 1) * bt + n) % rt
            at = i * ct + block * bt
            lhs = jnp.concatenate([tiles[tab[at + m]] for m in range(bt)], axis=1)
            y = dot(lhs, x[block])
            acc[i] = y if first else acc[i] + y
            return carry
        lax.fori_loop(lo, hi, body, 0, unroll=2)

    groups = [[(step - nb, nb) for nb in range(lb) if 0 <= step - nb < la] for step in range(la + lb - 1)]
    early = max(1, len(groups) - 2)
    exchange1, exchange2 = [], []
    tail = []
    for g, group in enumerate(groups):
        places = [(na, nb, nearest(p, la, na), nearest(q, lb, nb)) for na, nb in group]
        for na, nb, s, t in places:
            if g > 0:
                arrive(place(s, t, core))
            forward(na, nb, s, t)
        if g == 0:
            fetch.wait()
        todo = [(place(s, t, core), False) for _, _, s, t in places]
        if cores == 2:
            todo += [(place(s, t, 1 - core), True) for _, _, s, t in places]
        acc = acc1 if g < early else acc2
        last = g == len(groups) - 1
        for n, (block, remote) in enumerate(todo):
            if remote:
                arrive(block)
            first = g in (0, early) and n == 0
            if last:
                multiply(block, acc, 0, rt - bt, first)
                tail.append((block, first))
            else:
                multiply(block, acc, 0, rt, first)
        if g == early - 1:
            for k in range(1, n_col):
                to = (col + k) % n_col
                copy = pltpu.make_async_remote_copy(
                    src_ref=acc1.at[pl.ds(to * bt, bt)], dst_ref=in1.at[k - 1], send_sem=s1.at[k - 1],
                    recv_sem=r1.at[k - 1], device_id={"col": to}, device_id_type=MESH)
                copy.start()
                exchange1.append(copy)
    for k in range(1, n_col):
        to = (col + k) % n_col
        out2[k - 1] = acc2[pl.ds(to * bt, bt)].astype(BF16)
        copy = pltpu.make_async_remote_copy(
            src_ref=out2.at[k - 1], dst_ref=in2.at[k - 1], send_sem=s2.at[k - 1],
            recv_sem=r2.at[k - 1], device_id={"col": to}, device_id_type=MESH)
        copy.start()
        exchange2.append(copy)
    for block, first in tail:
        multiply(block, acc2, rt - bt, rt, first)
    for cond, copy in started:
        when(cond, copy.wait_send)

    y = acc1[pl.ds(col * bt, bt)] + acc2[pl.ds(col * bt, bt)]
    for n, copy in enumerate(exchange1):
        copy.wait()
        y = y + in1[n]
    for n, copy in enumerate(exchange2):
        copy.wait()
        y = y + in2[n].astype(F32)
    y = y.reshape(bt * tile, tile)

    w = weight[...]
    hi, lo = split(y)
    logits[...] = dot(hi, w) + dot(lo, w)
    lab = labels[...]
    padded = -(-w.shape[1] // tile) * tile
    onehot = (lax.broadcasted_iota(jnp.int32, (padded, bt * tile), 0) == lab).astype(F32).astype(BF16)
    picked = dot(onehot, hi) + dot(onehot, lo)
    hi_t, lo_t = split(y.T * jnp.where(lab >= 0, 1.0, 0.0).astype(F32))
    gram_hi, gram_lo = split(dot(hi_t, hi) + dot(hi_t, lo) + dot(lo_t, hi))
    total = dot(gram_hi, w) + dot(gram_lo, w) - picked.T[:, : w.shape[1]]
    wgrad[...] = total * scale


def local(n_row, n_col, features, weight, labels, tile_rows, tile_cols, tile_count, tile_vals):
    la, lb, cores = factors(n_row)
    classes, tile, slots = weight.shape[1], tile_vals.shape[-1], tile_vals.shape[2]
    own, feat = features.shape
    bt = own // tile
    rt, ct = n_col * bt, n_row * bt
    nodes = own * n_row * n_col
    key = jnp.where(jnp.arange(slots, dtype=jnp.int32) < tile_count.reshape(()),
                    tile_rows.reshape(slots) * ct + tile_cols.reshape(slots), -1)
    match = key[:, None] == jnp.arange(rt * ct, dtype=jnp.int32)[None, :]
    table = slots + jnp.sum(jnp.where(match, jnp.arange(slots, dtype=jnp.int32)[:, None] - slots, 0), axis=0)
    dims = (n_row, n_col, la, lb, cores, 1.0 / math.sqrt(nodes))
    vmem = pl.BlockSpec(memory_space=pltpu.VMEM)
    dma = pltpu.SemaphoreType.DMA
    peers = max(1, n_col - 1)
    logits, wgrad = pl.pallas_call(
        functools.partial(kernel, dims),
        out_shape=(jax.ShapeDtypeStruct((own, classes), F32), jax.ShapeDtypeStruct((feat, classes), F32)),
        in_specs=[vmem, vmem, vmem, pl.BlockSpec(memory_space=pltpu.SMEM), pl.BlockSpec(memory_space=pl.ANY)],
        out_specs=(vmem, vmem),
        scratch_shapes=[
            pltpu.VMEM((n_row, own, feat), BF16),
            pltpu.VMEM((slots + 1, tile, tile), BF16),
            pltpu.VMEM((rt, tile, feat), F32),
            pltpu.VMEM((rt, tile, feat), F32),
            pltpu.VMEM((peers, bt, tile, feat), BF16),
            pltpu.VMEM((peers, bt, tile, feat), F32),
            pltpu.VMEM((peers, bt, tile, feat), BF16),
            dma((la * lb, 5)), dma((n_row,)), dma(()),
            dma((peers,)), dma((peers,)), dma((peers,)), dma((peers,)),
        ],
        compiler_params=pltpu.CompilerParams(collective_id=0, has_side_effects=True, vmem_limit_bytes=48 * 2**20),
        cost_estimate=pl.CostEstimate(flops=2 * rt * ct * tile * tile * feat, bytes_accessed=slots * tile * tile * 2, transcendentals=0),
        name="aggregate",
    )(features, weight, labels.reshape(1, own), table, tile_vals.reshape(slots, tile, tile))
    return logits, lax.psum(wgrad, ("row", "col"))


def solution(mesh):
    placed = (
        P(("col", "row"), None),
        P(),
        P(("row", "col")),
        P("row", "col", None),
        P("row", "col", None),
        P("row", "col"),
        P("row", "col", None, None, None),
    )
    body = functools.partial(local, mesh.shape["row"], mesh.shape["col"])
    return jax.shard_map(
        body, mesh=mesh, in_specs=placed, out_specs=(P(("row", "col"), None), P()), check_vma=False
    )
```

time: 523 us -> 174 us (0.33)
  waiting for transfers between devices: 392 us -> 120 us
  other arithmetic: 45.6 us -> 0.86 us
  local copies, waits for them, and re-layouts: 38.4 us -> 5.03 us
  Pallas kernels: 0 us -> 33.2 us
  matrix products: 23.1 us -> 0 us
  blocking collectives: 6.97 us -> 0 us
    reduce_scatter x2 -> x0, waiting for transfers between devices: 220 us -> none  [the longest x1 143 us: local(): lax.psum_scatter(back.reshape(-1, classes), 'row', scatter_dimension=0, t...]
    all_gather x1 -> x0, waiting for transfers between devices: 48.6 us -> none  [local(): xw_full = lax.all_gather(local_xw, 'row', axis=0, tiled=True)]
    scatter-add x6 -> x0, other arithmetic: 37.5 us -> none  [step(): return acc.at[sidx].add(prod * valid[:, None, None])]
    pallas_call x0 -> x1, Pallas kernels: none -> 33.2 us  [local(): pl.pallas_call(functools.partial(kernel, dims), out_shape=(jax.ShapeDtype...]
    dot_general x9 -> x0, matrix products: 23.1 us -> none  [the longest x3 11 us: step(): jnp.einsum('tij,tjc->tic', piece, sel, preferred_element_type=jnp.float32)]
    gather x6 -> x0, local copies, waits for them, and re-layouts: 14.6 us -> none  [step(): sel = table[gidx]]
    while x4 -> x0, local copies, waits for them, and re-layouts: 10.7 us -> none  [aggregate(): return lax.fori_loop(0, nblk, step, init)]
    all_gather x1 -> x0, blocking collectives: 6.97 us -> none  [local(): loss_full = lax.all_gather(residual_grad, 'col', axis=0, tiled=True)]
  transfers between devices with their start and end apart: 4 -> 1, of which waited for: 4 -> 1; matrix products, arithmetic and copies ran while one was open for 0% -> 1% of each run, Pallas kernels for 0% -> 0%
where the time goes in v1:
time: 174 us
  waiting for transfers between devices  120 us (69%)
  Pallas kernels  33.2 us (19%)
  between operations  14.7 us (8%)
  local copies, waits for them, and re-layouts  5.03 us (3%)
    psum x1, waiting for transfers between devices, local(): return (logits, lax.psum(wgrad, ('row', 'col')))  120 us
    pallas_call x1, Pallas kernels, local(): pl.pallas_call(functools.partial(kernel, dims), out_shape=(jax.ShapeDtype...  33.2 us
    unnamed x7, local copies, waits for them, and re-layouts  5.03 us
  transfers between devices with their start and end apart: 1, of which 1 were waited for; matrix products, arithmetic and copies ran while one was open for 1% of the time, Pallas kernels for 0%

profile of v1, /device:TPU:0, one launch (start us, length us, event | category | flops | bytes accessed | tf_op | source)
XLA Modules:
  0.0 173.7 jit_solution(7855542936032277859)
XLA Ops:
  7.2 0.0 all-reduce.2.cloned.1.call-start
  7.9 0.7 multiply_add_fusion
  8.6 0.1 select_reduce_fusion
  8.7 0.9 copy.12.weight
  9.6 0.0 copy-start
  9.6 0.9 copy-done
  10.5 0.0 copy-start.1
  10.5 0.7 copy-done.1
  11.2 33.2 %aggregate.1 = (f32[512,172]{1,0:T(8,128)S(1)}, f32[128,172]{1,0:T(8,128)}) custom-call(bf16[512,128]{1,0:T(8,128)(2,1)S(1)} %copy-done, bf16[128,172]{1,0:T(8,128)(2,1)S(1)} %copy.12.weight, s32[1,512]{1,0:T(1,128)S(1)} %bitcast.5, s32[512]{0:T(512)S(1)} %broadcast_add_fusion.tab, bf16[256,128,128]{2,1,0:T(8,128)(2,1)} %bitcast.6), custom_call_target="tpu_custom_call" | custom-call | flops 2147483648 | bytes 8388608 | tf_op jit(solution)/shard_map/aggregate/pallas_call | solution.py:202
  44.4 0.0 all-reduce.2.cloned.1.call-update
  44.4 0.9 copy.13
  45.4 119.8 %all-reduce.2.cloned.1.call-done = f32[128,172]{1,0:T(8,128)} async-done(((f32[128,172]{1,0:T(8,128)}), f32[128,172]{1,0:T(8,128)}) %all-reduce.2.cloned.1.call-update) | async-done | bytes 88080 | tf_op jit(solution)/shard_map/psum | solution.py:222
  165.2 1.6 copy.14
  (2 shorter events, 0.0 us)
Async XLA Ops:
  7.2 158.0 %all-reduce.2.cloned.1.call-start = ((), (), s32[]{:S(2)}) async-start(), calls=%async_computation | async-start | bytes 262144 | tf_op jit(solution)/shard_map/psum | solution.py:222
  9.6 0.9 copy-start
  10.5 0.7 copy-start.1
Sparse Core Ops, SparseCore 0:
  44.6 120.5 all-reduce.1
